TPU v7x, 32 devices: a whole 2x2x4 slice. The times are simulated.
32 devices in a mesh: col: 8 (over z, y), row: 4 (over x, core).
Axes of the slice: x: 2, y: 2, z: 4, core: 2. Of those that a mesh axis runs over, the one named last changes fastest.
Arguments:
- u_factors: bfloat16 [2, 64, 256, 64, 128], P(None, 'row', None, 'col'), may hold values from -0.09375 to 0.09375
- v_factors: bfloat16 [2, 64, 256, 64, 128], P(None, 'row', None, 'col'), may hold values from -0.375 to 0.375
- ranks: int32 [2, 64, 64], P(None, 'row', 'col'), may hold values from 8 to 64
- model_init: float32 [2, 16384, 256], P(None, ('col', 'row')), may hold values from -6 to 6
- observed: float32 [2, 16384, 256], P(None, ('row', 'col')), may hold values from -6 to 6
- step: float32 [2], replicated, may hold values from 0.1 to 0.4
Outputs:
- model: float32 [2, 16384, 256], P(None, ('col', 'row'))
- misfit: float32 [2, 16384, 256], P(None, ('row', 'col'))
Inputs may be any that keep to these rules, and one draw needn't show every extreme that they name: `ranks`: columns of a factor beyond its tile's rank do not count.
All inputs are finite; a program needn't handle non-finite values.
Results may differ from a plain program's by a relative error of at most 0.0085.
Values may be sent and summed in bfloat16 or wider, within the bound.
No kernel may reach another device: no remote copies, remote signals or barrier semaphores. Data moves between devices by JAX's collectives and lax.ppermute only.
A program may use at most 192 MiB of HBM per device.

v0:
```python
import jax
import jax.numpy as jnp
from jax import lax
from jax.sharding import PartitionSpec as P

ITERS = 2


def split_product(product, rank_mask, rank_most, right_count):
    real = product[..., :rank_most, :right_count] + product[..., rank_most:, right_count:]
    imaginary = product[..., :rank_most, right_count:] - product[..., rank_most:, :right_count]
    weights = rank_mask[..., None]
    return jnp.concatenate([real * weights, imaginary * weights], -1).astype(jnp.bfloat16)


def expand_complex(coefficient, right_count):
    real = coefficient[..., :right_count]
    imaginary = coefficient[..., right_count:]
    upper = jnp.concatenate([real, imaginary], -1)
    lower = jnp.concatenate([-imaginary, real], -1)
    return jnp.concatenate([upper, lower], -2)


def local(u_factors, v_factors, ranks, model_init, observed, step):
    frequencies = model_init.shape[0]
    rank_most = u_factors.shape[-1] // 2
    right_count = model_init.shape[-1] // 2
    tile_size = u_factors.shape[2]
    rows_here = u_factors.shape[1]
    cols_here = u_factors.shape[3]
    rank_mask = (
        jnp.arange(rank_most, dtype=jnp.int32)[None, None, None, :] < ranks[..., None]
    ).astype(jnp.float32)
    model = model_init
    misfit = model_init
    for sweep in range(ITERS):
        gathered = lax.all_gather(model.astype(jnp.bfloat16), "row", axis=1, tiled=True)
        model_tiles = gathered.reshape(frequencies, cols_here, tile_size, 2 * right_count)
        product = jnp.einsum(
            "fiajk,fjal->fijkl", v_factors, model_tiles, preferred_element_type=jnp.float32
        )
        coefficient = expand_complex(
            split_product(product, rank_mask, rank_most, right_count), right_count
        )
        partial_value = jnp.einsum(
            "fiajk,fijkl->fial", u_factors, coefficient, preferred_element_type=jnp.float32
        )
        partial_value = partial_value.reshape(frequencies, rows_here * tile_size, 2 * right_count)
        predicted = lax.psum_scatter(partial_value, "col", scatter_dimension=1, tiled=True)
        misfit = predicted - observed
        misfit_half = lax.all_gather(misfit.astype(jnp.bfloat16), "col", axis=1, tiled=True)
        misfit_tiles = misfit_half.reshape(frequencies, rows_here, tile_size, 2 * right_count)
        product = jnp.einsum(
            "fiajk,fial->fijkl", u_factors, misfit_tiles, preferred_element_type=jnp.float32
        )
        back = expand_complex(
            split_product(product, rank_mask, rank_most, right_count), right_count
        )
        gradient_part = jnp.einsum(
            "fiajk,fijkl->fjal", v_factors, back, preferred_element_type=jnp.float32
        )
        gradient_part = gradient_part.reshape(frequencies, cols_here * tile_size, 2 * right_count)
        gradient = lax.psum_scatter(gradient_part, "row", scatter_dimension=1, tiled=True)
        model = model - step[:, None, None] * gradient
    return (model, misfit)


def solution(mesh):
    return jax.shard_map(
        local,
        mesh=mesh,
        in_specs=(
            P(None, "row", None, "col", None),
            P(None, "row", None, "col", None),
            P(None, "row", "col"),
            P(None, ("col", "row"), None),
            P(None, ("row", "col"), None),
            P(),
        ),
        out_specs=(P(None, ("col", "row"), None), P(None, ("row", "col"), None)),
        check_vma=False,
    )
```

profile of v0, /device:TPU:0, one launch (start us, length us, event | category | flops | bytes accessed | tf_op | source)
XLA Modules:
  0.0 867.7 jit_solution(3654112159293846714)
XLA Ops:
  9.4 23.4 %copy.11 = bf16[2,16,256,8,128]{2,4,3,1,0:T(8,128)(2,1)} copy(bf16[2,16,256,8,128]{4,3,2,1,0:T(8,128)(2,1)} %param.6) | data formatting | bytes 33554432 | tf_op args[0]
  32.8 23.6 %copy.8 = bf16[2,16,256,8,128]{2,4,1,3,0:T(8,128)(2,1)} copy(bf16[2,16,256,8,128]{4,3,2,1,0:T(8,128)(2,1)} %param.7) | data formatting | bytes 33554432 | tf_op args[1]
  56.5 17.2 %fusion.49 = f32[2,8,256,2048]{2,3,1,0} fusion(bf16[2,8,256,2048]{2,3,1,0:T(8,128)(2,1)} %bitcast.61, bf16[2,8,256,256]{3,2,1,0:T(8,128)(2,1)} %bitcast.85), kind=kOutput, calls=%fused_computation.61 | convolution fusion | flops 4294967296 | bytes 52428800
  81.2 9.2 %fusion.47 = (bf16[2,16,8,64,128]{4,3,1,2,0:T(8,128)(2,1)S(1)}, bf16[2,16,8,64,128]{4,3,1,2,0:T(8,128)(2,1)}) fusion(f32[2,16,8,64]{3,1,2,0:T(8,128)S(1)} %fusion.37, f32[2,16,8,128,256]{4,3,1,2,0:T(8,128)} %bitcast.70), kind=kLoop, calls=%fused_computation.60 | loop fusion | flops 8388608 | bytes 25231360 | tf_op jit(solution)/shard_map/neg | solution.py:20
  90.4 12.2 %fusion.18 = f32[2,16,256,256,1]{2,3,4,1,0:T(8,128)} fusion(bf16[2,16,256,8,128]{2,4,3,1,0:T(8,128)(2,1)} %copy.11, bf16[2,16,8,64,128]{4,3,1,2,0:T(8,128)(2,1)S(1)} %fusion.35, bf16[2,16,8,64,128]{4,3,1,2,0:T(8,128)(2,1)S(1)} %get-tuple-element.10, bf16[2,16,8,64,128]{4,3,1,2,0:T(8,128)(2,1)} %get-tuple-element.11), kind=kOutput, calls=%fused_computation.22 | convolution fusion | flops 4362076160 | bytes 37748736 | tf_op jit(solution)/shard_map/fiajk,fijkl->fial/dot_general | solution.py:45
  102.6 151.8 %reduce-scatter.5.cloned.1.call-done = f32[2,512,256]{2,1,0:T(8,128)} async-done(((f32[2,4096,256]{2,1,0:T(8,128)}), f32[2,512,256]{2,1,0:T(8,128)}) %reduce-scatter.5.cloned.1.call-update) | async-done | bytes 1048592 | tf_op jit(solution)/shard_map/reduce_scatter | solution.py:49
  256.8 73.0 %all-gather.7.cloned.1.call-done = bf16[2,4096,256]{2,1,0:T(8,128)(2,1)} async-done(((bf16[2,512,256]{2,1,0:T(8,128)(2,1)}), bf16[2,4096,256]{2,1,0:T(8,128)(2,1)}) %all-gather.7.cloned.1.call-update) | async-done | bytes 4194320 | tf_op jit(solution)/shard_map/all_gather | solution.py:51
  329.8 17.7 %fusion.50 = f32[2,16,256,1024]{2,3,1,0} fusion(bf16[2,16,256,1024]{2,3,1,0:T(8,128)(2,1)} %bitcast.67, bf16[2,16,256,256]{3,2,1,0:T(8,128)(2,1)} %bitcast.82), kind=kOutput, calls=%fused_computation.62 | convolution fusion | flops 4294967296 | bytes 54525952
  347.5 22.9 %copy.31 = f32[2,16,256,8,128]{2,4,1,3,0:T(8,128)} copy(f32[2,16,256,8,128]{2,4,3,1,0:T(8,128)} %bitcast.74) | data formatting | bytes 67108864 | tf_op jit(solution)/shard_map/fiajk,fial->fijkl/dot_general | solution.py:53
  370.4 10.7 %fusion.31 = bf16[2,16,8,64,128]{4,3,1,2,0:T(8,128)(2,1)} fusion(f32[2,16,8,128,256]{4,3,1,2,0:T(8,128)} %bitcast.77, f32[2,16,8,64]{3,1,2,0:T(8,128)S(1)} %fusion.37), kind=kLoop, calls=%fused_computation.41 | loop fusion | flops 6291456 | bytes 21037056 | tf_op jit(solution)/shard_map/slice | solution.py:17
  381.0 11.1 %fusion.45 = (bf16[2,16,8,64,128]{4,3,1,2,0:T(8,128)(2,1)}, bf16[2,16,8,64,128]{4,3,1,2,0:T(8,128)(2,1)}) fusion(f32[2,16,8,64]{3,1,2,0:T(8,128)S(1)} %fusion.37, f32[2,16,8,128,256]{4,3,1,2,0:T(8,128)} %bitcast.78), kind=kLoop, calls=%fused_computation.59 | loop fusion | flops 8388608 | bytes 25231360 | tf_op jit(solution)/shard_map/neg | solution.py:20
  392.3 11.0 %fusion = f32[2,8,256,256,1]{2,3,4,1,0:T(8,128)} fusion(bf16[2,16,256,8,128]{2,4,1,3,0:T(8,128)(2,1)S(1)} %bitcast.64, bf16[2,16,8,64,128]{4,3,1,2,0:T(8,128)(2,1)} %fusion.31, bf16[2,16,8,64,128]{4,3,1,2,0:T(8,128)(2,1)} %get-tuple-element.8, bf16[2,16,8,64,128]{4,3,1,2,0:T(8,128)(2,1)} %get-tuple-element.9), kind=kOutput, calls=%fused_computation.3 | convolution fusion | flops 4362076160 | bytes 33554432 | tf_op jit(solution)/shard_map/fiajk,fijkl->fjal/dot_general | solution.py:59
  403.4 42.9 %reduce-scatter.7.cloned.1.call-done = f32[2,512,256]{2,1,0:T(8,128)} async-done(((f32[2,2048,256]{2,1,0:T(8,128)}), f32[2,512,256]{2,1,0:T(8,128)}) %reduce-scatter.7.cloned.1.call-update) | async-done | bytes 1048592 | tf_op jit(solution)/shard_map/reduce_scatter | solution.py:63
  448.6 22.7 %all-gather.9.cloned.1.call-done = bf16[2,2048,256]{2,1,0:T(8,128)(2,1)} async-done(((bf16[2,512,256]{2,1,0:T(8,128)(2,1)}), bf16[2,2048,256]{2,1,0:T(8,128)(2,1)}) %all-gather.9.cloned.1.call-update) | async-done | bytes 2097168 | tf_op jit(solution)/shard_map/all_gather | solution.py:37
  471.3 17.1 %fusion.51 = f32[2,8,256,2048]{2,3,1,0} fusion(bf16[2,8,256,2048]{2,3,1,0:T(8,128)(2,1)} %bitcast.62, bf16[2,8,256,256]{3,2,1,0:T(8,128)(2,1)} %bitcast.86), kind=kOutput, calls=%fused_computation.63 | convolution fusion | flops 4294967296 | bytes 52428800
  505.1 12.2 %fusion.16 = f32[2,16,256,256,1]{2,3,4,1,0:T(8,128)} fusion(bf16[2,16,256,8,128]{2,4,3,1,0:T(8,128)(2,1)} %copy.11, bf16[2,16,8,64,128]{4,3,1,2,0:T(8,128)(2,1)S(1)} %fusion.27, bf16[2,16,8,64,128]{4,3,1,2,0:T(8,128)(2,1)S(1)} %get-tuple-element.6, bf16[2,16,8,64,128]{4,3,1,2,0:T(8,128)(2,1)} %get-tuple-element.7), kind=kOutput, calls=%fused_computation.20 | convolution fusion | flops 4362076160 | bytes 37748736 | tf_op jit(solution)/shard_map/fiajk,fijkl->fial/dot_general | solution.py:45
  517.4 149.2 %reduce-scatter.9.cloned.1.call-done = f32[2,512,256]{2,1,0:T(8,128)} async-done(((f32[2,4096,256]{2,1,0:T(8,128)}), f32[2,512,256]{2,1,0:T(8,128)}) %reduce-scatter.9.cloned.1.call-update) | async-done | bytes 1048592 | tf_op jit(solution)/shard_map/reduce_scatter | solution.py:49
  669.4 72.6 %all-gather.11.cloned.1.call-done = bf16[2,4096,256]{2,1,0:T(8,128)(2,1)} async-done(((bf16[2,512,256]{2,1,0:T(8,128)(2,1)}), bf16[2,4096,256]{2,1,0:T(8,128)(2,1)}) %all-gather.11.cloned.1.call-update) | async-done | bytes 4194320 | tf_op jit(solution)/shard_map/all_gather | solution.py:51
  741.9 17.7 %fusion.52 = f32[2,16,256,1024]{2,3,1,0} fusion(bf16[2,16,256,1024]{2,3,1,0:T(8,128)(2,1)} %bitcast.68, bf16[2,16,256,256]{3,2,1,0:T(8,128)(2,1)} %bitcast.81), kind=kOutput, calls=%fused_computation.64 | convolution fusion | flops 4294967296 | bytes 54525952
  759.6 22.9 %copy.30 = f32[2,16,256,8,128]{2,4,1,3,0:T(8,128)} copy(f32[2,16,256,8,128]{2,4,3,1,0:T(8,128)} %bitcast.73) | data formatting | bytes 67108864 | tf_op jit(solution)/shard_map/fiajk,fial->fijkl/dot_general | solution.py:53
  782.5 10.7 %fusion.23 = bf16[2,16,8,64,128]{4,3,1,2,0:T(8,128)(2,1)} fusion(f32[2,16,8,128,256]{4,3,1,2,0:T(8,128)} %bitcast.75, f32[2,16,8,64]{3,1,2,0:T(8,128)S(1)} %fusion.37), kind=kLoop, calls=%fused_computation.29 | loop fusion | flops 6291456 | bytes 21037056 | tf_op jit(solution)/shard_map/slice | solution.py:17
  793.2 11.1 %fusion.40 = (bf16[2,16,8,64,128]{4,3,1,2,0:T(8,128)(2,1)}, bf16[2,16,8,64,128]{4,3,1,2,0:T(8,128)(2,1)}) fusion(f32[2,16,8,64]{3,1,2,0:T(8,128)S(1)} %fusion.37, f32[2,16,8,128,256]{4,3,1,2,0:T(8,128)} %bitcast.76), kind=kLoop, calls=%fused_computation.56 | loop fusion | flops 8388608 | bytes 25231360 | tf_op jit(solution)/shard_map/neg | solution.py:20
  804.4 11.0 %fusion.8 = f32[2,8,256,256,1]{2,3,4,1,0:T(8,128)} fusion(bf16[2,16,256,8,128]{2,4,1,3,0:T(8,128)(2,1)S(1)} %bitcast.66, bf16[2,16,8,64,128]{4,3,1,2,0:T(8,128)(2,1)} %fusion.23, bf16[2,16,8,64,128]{4,3,1,2,0:T(8,128)(2,1)} %get-tuple-element.2, bf16[2,16,8,64,128]{4,3,1,2,0:T(8,128)(2,1)} %get-tuple-element.3), kind=kOutput, calls=%fused_computation.12 | convolution fusion | flops 4362076160 | bytes 33554432 | tf_op jit(solution)/shard_map/fiajk,fijkl->fjal/dot_general | solution.py:59
  815.4 42.9 %reduce-scatter.11.cloned.1.call-done = f32[2,512,256]{2,1,0:T(8,128)} async-done(((f32[2,2048,256]{2,1,0:T(8,128)}), f32[2,512,256]{2,1,0:T(8,128)}) %reduce-scatter.11.cloned.1.call-update) | async-done | bytes 1048592 | tf_op jit(solution)/shard_map/reduce_scatter | solution.py:63
  (54 shorter events, 36.8 us)
Async XLA Ops:
  7.2 49.4 %all-gather.5.cloned.1.call-start = ((), (), s32[]{:S(2)}) async-start(), calls=%async_computation.4 | async-start | bytes 2621440 | tf_op jit(solution)/shard_map/all_gather | solution.py:37
  9.3 245.1 %reduce-scatter.5.cloned.1.call-start = ((), (), s32[]{:S(2)}) async-start(), calls=%async_computation.5 | async-start | bytes 9437184 | tf_op jit(solution)/shard_map/reduce_scatter | solution.py:49
  32.8 23.6 %copy-start.3 = (s32[2,16,8]{1,2,0:T(8,128)S(1)}, s32[2,16,8]{1,2,0:T(8,128)}, u32[]{:S(2)}) copy-start(s32[2,16,8]{1,2,0:T(8,128)} %param.8) | copy-start | bytes 3076
  102.5 151.8 %copy-start.1 = (f32[2,512,256]{2,1,0:T(8,128)S(1)}, f32[2,512,256]{2,1,0:T(8,128)}, u32[]{:S(2)}) copy-start(f32[2,512,256]{2,1,0:T(8,128)} %param.10) | copy-start | bytes 3145732
  102.6 227.2 %all-gather.7.cloned.1.call-start = ((), (), s32[]{:S(2)}) async-start(), calls=%async_computation.6 | async-start | bytes 4718592 | tf_op jit(solution)/shard_map/all_gather | solution.py:51
  256.6 189.6 %reduce-scatter.7.cloned.1.call-start = ((), (), s32[]{:S(2)}) async-start(), calls=%async_computation.7 | async-start | bytes 5242880 | tf_op jit(solution)/shard_map/reduce_scatter | solution.py:63
  370.4 21.8 %slice-start = ((s8[16777216]{0:T(1024)(128)(4,1)}), s8[4194304]{0:T(1024)(128)(4,1)S(1)}, s32[]{:S(2)}) async-start(s8[16777216]{0:T(1024)(128)(4,1)} %bitcast.63), calls=%async_computation.12 | async-start | bytes 8388608
  370.4 21.8 %slice-start.1 = ((s8[16777216]{0:T(1024)(128)(4,1)}), s8[4194304]{0:T(1024)(128)(4,1)S(1)}, s32[]{:S(2)}) async-start(s8[16777216]{0:T(1024)(128)(4,1)} %bitcast.63), calls=%async_computation.13 | async-start | bytes 8388608
  381.0 11.2 %slice-start.2 = ((s8[16777216]{0:T(1024)(128)(4,1)}), s8[4194304]{0:T(1024)(128)(4,1)S(1)}, s32[]{:S(2)}) async-start(s8[16777216]{0:T(1024)(128)(4,1)} %bitcast.63), calls=%async_computation.14 | async-start | bytes 8388608
  381.0 11.2 %slice-start.3 = ((s8[16777216]{0:T(1024)(128)(4,1)}), s8[4194304]{0:T(1024)(128)(4,1)S(1)}, s32[]{:S(2)}) async-start(s8[16777216]{0:T(1024)(128)(4,1)} %bitcast.63), calls=%async_computation.15 | async-start | bytes 8388608
  392.2 54.0 %copy-start = (f32[2,512,256]{2,1,0:T(8,128)S(1)}, f32[2,512,256]{2,1,0:T(8,128)}, u32[]{:S(2)}) copy-start(f32[2,512,256]{2,1,0:T(8,128)} %param.9) | copy-start | bytes 3145732
  392.2 54.0 %copy-start.4 = (f32[2]{0:T(128)S(1)}, f32[2]{0:T(128)}, u32[]{:S(2)}) copy-start(f32[2]{0:T(128)} %param.11) | copy-start | bytes 28
  403.3 68.0 %all-gather.9.cloned.1.call-start = ((), (), s32[]{:S(2)}) async-start(), calls=%async_computation.8 | async-start | bytes 2621440 | tf_op jit(solution)/shard_map/all_gather | solution.py:37
  448.5 218.0 %reduce-scatter.9.cloned.1.call-start = ((), (), s32[]{:S(2)}) async-start(), calls=%async_computation.9 | async-start | bytes 9437184 | tf_op jit(solution)/shard_map/reduce_scatter | solution.py:49
  517.3 224.6 %all-gather.11.cloned.1.call-start = ((), (), s32[]{:S(2)}) async-start(), calls=%async_computation.10 | async-start | bytes 4718592 | tf_op jit(solution)/shard_map/all_gather | solution.py:51
  669.1 189.2 %reduce-scatter.11.cloned.1.call-start = ((), (), s32[]{:S(2)}) async-start(), calls=%async_computation.11 | async-start | bytes 5242880 | tf_op jit(solution)/shard_map/reduce_scatter | solution.py:63
  782.5 21.8 %slice-start.4 = ((s8[16777216]{0:T(1024)(128)(4,1)}), s8[4194304]{0:T(1024)(128)(4,1)S(1)}, s32[]{:S(2)}) async-start(s8[16777216]{0:T(1024)(128)(4,1)} %bitcast.65), calls=%async_computation.16 | async-start | bytes 8388608
  782.5 21.8 %slice-start.5 = ((s8[16777216]{0:T(1024)(128)(4,1)}), s8[4194304]{0:T(1024)(128)(4,1)S(1)}, s32[]{:S(2)}) async-start(s8[16777216]{0:T(1024)(128)(4,1)} %bitcast.65), calls=%async_computation.17 | async-start | bytes 8388608
  793.2 11.2 %slice-start.6 = ((s8[16777216]{0:T(1024)(128)(4,1)}), s8[4194304]{0:T(1024)(128)(4,1)S(1)}, s32[]{:S(2)}) async-start(s8[16777216]{0:T(1024)(128)(4,1)} %bitcast.65), calls=%async_computation.18 | async-start | bytes 8388608
  793.2 11.2 %slice-start.7 = ((s8[16777216]{0:T(1024)(128)(4,1)}), s8[4194304]{0:T(1024)(128)(4,1)S(1)}, s32[]{:S(2)}) async-start(s8[16777216]{0:T(1024)(128)(4,1)} %bitcast.65), calls=%async_computation.19 | async-start | bytes 8388608
  804.3 54.0 %copy-start.2 = (f32[2,512,256]{2,1,0:T(8,128)S(1)}, f32[2,512,256]{2,1,0:T(8,128)}, u32[]{:S(2)}) copy-start(f32[2,512,256]{2,1,0:T(8,128)} %reduce-scatter.7.cloned.1.call-done) | copy-start | bytes 3145732
Sparse Core Ops, SparseCore 0:
  10.1 25.2 all-gather.4
  102.7 151.6 reduce-scatter.4
  257.4 72.3 all-gather.6
  403.4 42.7 reduce-scatter.6
  448.7 22.5 all-gather.8
  517.4 149.0 reduce-scatter.8
  669.5 72.3 all-gather.10
  815.5 42.7 reduce-scatter.10
where the time goes:
time: 869 us; the launch traced here: 868 us
  waiting for transfers between devices  555 us (64%)
  matrix products  116 us (13%)
  local copies, waits for them, and re-layouts  92.9 us (11%)
  other arithmetic  88.6 us (10%)
  between operations  14.3 us (2%)
    reduce_scatter x2, waiting for transfers between devices, local(): lax.psum_scatter(partial_value, 'col', scatter_dimension=1, tiled=True)  301 us
    all_gather x2, waiting for transfers between devices, local(): lax.all_gather(misfit.astype(jnp.bfloat16), 'col', axis=1, tiled=True)  146 us
    reduce_scatter x2, waiting for transfers between devices, local(): lax.psum_scatter(gradient_part, 'row', scatter_dimension=1, tiled=True)  85.8 us
    unnamed x4, matrix products  69.6 us
    unnamed x28, local copies, waits for them, and re-layouts  47.1 us
    dot_general x2, local copies, waits for them, and re-layouts, local(): jnp.einsum('fiajk,fial->fijkl', u_factors, misfit_tiles, preferred_elemen...  45.8 us
    neg x4, other arithmetic, expand_complex(): lower = jnp.concatenate([-imaginary, real], -1)  40.7 us
    slice x4, other arithmetic, expand_complex(): real = coefficient[..., :right_count]  36.2 us
  transfers between devices with their start and end apart: 8, of which 7 were waited for; matrix products, arithmetic and copies ran while one was open for 5% of the time, Pallas kernels for 0%

commit v1 on v0

v1 whole, which is shorter than its diff:
```python
import functools

import jax
import jax.numpy as jnp
from jax import lax
from jax.experimental import pallas as pl
from jax.experimental.pallas import tpu as pltpu
from jax.sharding import PartitionSpec as P

ITERS = 2
GROUPS = 1
VMEM = 48 << 20
F32 = jnp.float32
BF16 = jnp.bfloat16
CONTRACT_FIRST = (((0,), (0,)), ((), ()))


def split_product(product, rank_mask, rank_most, right_count):
    real = product[..., :rank_most, :right_count] + product[..., rank_most:, right_count:]
    imaginary = product[..., :rank_most, right_count:] - product[..., rank_most:, :right_count]
    weights = rank_mask[..., None]
    return jnp.concatenate([real * weights, imaginary * weights], -1).astype(BF16)


def expand_complex(coefficient, right_count):
    real = coefficient[..., :right_count]
    imaginary = coefficient[..., right_count:]
    upper = jnp.concatenate([real, imaginary], -1)
    lower = jnp.concatenate([-imaginary, real], -1)
    return jnp.concatenate([upper, lower], -2)


def local_plain(u_factors, v_factors, ranks, model_init, observed, step):
    frequencies = model_init.shape[0]
    rank_most = u_factors.shape[-1] // 2
    right_count = model_init.shape[-1] // 2
    tile_size = u_factors.shape[2]
    rows_here = u_factors.shape[1]
    cols_here = u_factors.shape[3]
    rank_mask = (
        jnp.arange(rank_most, dtype=jnp.int32)[None, None, None, :] < ranks[..., None]
    ).astype(F32)
    model = model_init
    misfit = model_init
    for sweep in range(ITERS):
        gathered = lax.all_gather(model.astype(BF16), "row", axis=1, tiled=True)
        model_tiles = gathered.reshape(frequencies, cols_here, tile_size, 2 * right_count)
        product = jnp.einsum("fiajk,fjal->fijkl", v_factors, model_tiles, preferred_element_type=F32)
        coefficient = expand_complex(split_product(product, rank_mask, rank_most, right_count), right_count)
        partial_value = jnp.einsum("fiajk,fijkl->fial", u_factors, coefficient, preferred_element_type=F32)
        partial_value = partial_value.reshape(frequencies, rows_here * tile_size, 2 * right_count)
        predicted = lax.psum_scatter(partial_value, "col", scatter_dimension=1, tiled=True)
        misfit = predicted - observed
        misfit_half = lax.all_gather(misfit.astype(BF16), "col", axis=1, tiled=True)
        misfit_tiles = misfit_half.reshape(frequencies, rows_here, tile_size, 2 * right_count)
        product = jnp.einsum("fiajk,fial->fijkl", u_factors, misfit_tiles, preferred_element_type=F32)
        back = expand_complex(split_product(product, rank_mask, rank_most, right_count), right_count)
        gradient_part = jnp.einsum("fiajk,fijkl->fjal", v_factors, back, preferred_element_type=F32)
        gradient_part = gradient_part.reshape(frequencies, cols_here * tile_size, 2 * right_count)
        gradient = lax.psum_scatter(gradient_part, "row", scatter_dimension=1, tiled=True)
        model = model - step[:, None, None] * gradient
    return (model, misfit)


def tile_columns(ref, lead):
    tiles = jnp.swapaxes(ref[lead], 0, 1)
    return [tiles[j] for j in range(tiles.shape[0])]


def combine(product, rank):
    half_k = product.shape[0] // 2
    half_r = product.shape[1] // 2
    kept = lax.broadcasted_iota(jnp.int32, (half_k, half_r), 0) < rank
    zero = jnp.zeros((half_k, half_r), F32)
    real = product[:half_k, :half_r] + product[half_k:, half_r:]
    imaginary = product[:half_k, half_r:] - product[half_k:, :half_r]
    real = jnp.where(kept, real, zero).astype(BF16)
    imaginary = jnp.where(kept, imaginary, zero).astype(BF16)
    upper = jnp.concatenate([real, imaginary], 1)
    lower = jnp.concatenate([-imaginary, real], 1)
    return jnp.concatenate([upper, lower], 0)


def fetches(place, u_hbm, v_hbm, u_buf, v_buf, sems, items, shards, first, v_first):
    rows = u_buf.shape[1]
    u_copies, v_copies = [], []
    for n, (g, s) in enumerate(items):
        where = pl.ds(place[shards[s]] * rows, rows)
        u_copies.append(pltpu.make_async_copy(u_hbm.at[first + g, where], u_buf.at[n], sems.at[0, n]))
        v_copies.append(pltpu.make_async_copy(v_hbm.at[first + g, where], v_buf.at[n], sems.at[1, n]))
    if v_first:
        for v_copy, u_copy in zip(v_copies, u_copies):
            v_copy.start()
            u_copy.start()
    else:
        for copy in u_copies + v_copies:
            copy.start()
    return u_copies, v_copies


def forward_kernel(place, ranks, x_ref, u_hbm, v_hbm, *rest, first, items, shards):
    outs, (u_buf, v_buf, sems) = rest[:-3], rest[-3:]
    rows, size, cols, width = u_buf.shape[1:]
    members, block = x_ref.shape[1:3]
    u_copies, v_copies = fetches(place, u_hbm, v_hbm, u_buf, v_buf, sems, items, shards, first, True)
    for n, (g, s) in enumerate(items):
        v_copies[n].wait()
        right = [tile_columns(v_buf, (n, i)) for i in range(rows)]
        coefficient = [[] for i in range(rows)]
        for j in range(cols):
            member, inside = divmod(j * size, block)
            product = lax.dot_general(
                jnp.concatenate([right[i][j] for i in range(rows)], 1),
                x_ref[g, place[place.shape[0] - 1] ^ member, inside : inside + size, :],
                CONTRACT_FIRST,
                preferred_element_type=F32,
            )
            for i in range(rows):
                rank = ranks[first + g, place[shards[s]] * rows + i, j]
                coefficient[i].append(combine(product[i * width : (i + 1) * width], rank))
        u_copies[n].wait()
        for i in range(rows):
            outs[s][g, i * size : (i + 1) * size, :] = jnp.dot(
                jnp.concatenate(tile_columns(u_buf, (n, i)), 1),
                jnp.concatenate(coefficient[i], 0),
                preferred_element_type=F32,
            ).astype(outs[s].dtype)


def adjoint_kernel(place, ranks, u_hbm, v_hbm, *rest, first, items, shards, fresh):
    count = max(s for g, s in items) + 1
    r_refs, (out_ref, u_buf, v_buf, sems) = rest[:count], rest[-4:]
    rows, size, cols, width = u_buf.shape[1:]
    u_copies, v_copies = fetches(place, u_hbm, v_hbm, u_buf, v_buf, sems, items, shards, first, False)
    back = []
    for n, (g, s) in enumerate(items):
        u_copies[n].wait()
        for i in range(rows):
            product = lax.dot_general(
                jnp.concatenate(tile_columns(u_buf, (n, i)), 1),
                r_refs[s][g, i * size : (i + 1) * size, :],
                CONTRACT_FIRST,
                preferred_element_type=F32,
            )
            back.append(
                [
                    combine(
                        product[j * width : (j + 1) * width], ranks[first + g, place[shards[s]] * rows + i, j]
                    )
                    for j in range(cols)
                ]
            )
    for copy in v_copies:
        copy.wait()
    for g in range(out_ref.shape[0]):
        mine = [(n, i) for n, item in enumerate(items) if item[0] == g for i in range(rows)]
        right = [tile_columns(v_buf, at) for at in mine]
        for j in range(cols):
            added = jnp.dot(
                jnp.concatenate([tiles[j] for tiles in right], 1),
                jnp.concatenate([back[n * rows + i][j] for n, i in mine], 0),
                preferred_element_type=F32,
            )
            where = slice(j * size, (j + 1) * size)
            if fresh:
                out_ref[g, where, :] = added
            else:
                out_ref[g, where, :] += added


VMEM_SPEC = pl.BlockSpec(memory_space=pltpu.VMEM)
SMEM_SPEC = pl.BlockSpec(memory_space=pltpu.SMEM)
HBM_SPEC = pl.BlockSpec(memory_space=pltpu.HBM)


def buffers(count, rows, factors):
    shape = (count, rows) + factors.shape[2:]
    return [pltpu.VMEM(shape, BF16), pltpu.VMEM(shape, BF16), pltpu.SemaphoreType.DMA((2, count))]


def cost(count, rows, factors):
    size, cols, width = factors.shape[2:]
    flops = 8 * count * rows * size * cols * width * size
    return pl.CostEstimate(flops=flops, bytes_accessed=4 * count * rows * size * cols * width, transcendentals=0)


def forward(u, v, x, ranks, place, shards, first, rows, dtype):
    group, lines = x.shape[0], x.shape[3]
    many = len(shards)
    shards = tuple(k % (place.shape[0] - 1) for k in shards)
    items = [(g, s) for g in range(group) for s in range(many)]
    out = jax.ShapeDtypeStruct((group, rows * u.shape[2], lines), dtype)
    return pl.pallas_call(
        functools.partial(forward_kernel, first=first, items=items, shards=shards),
        out_shape=[out] * many,
        in_specs=[SMEM_SPEC, SMEM_SPEC, VMEM_SPEC, HBM_SPEC, HBM_SPEC],
        out_specs=[VMEM_SPEC] * many,
        scratch_shapes=buffers(len(items), rows, u),
        compiler_params=pltpu.CompilerParams(vmem_limit_bytes=VMEM),
        cost_estimate=cost(len(items), rows, u),
    )(place, ranks, x, u, v)


def adjoint(u, v, arrived, ranks, start, place, shards, first, rows):
    group, lines = arrived[0].shape[0], arrived[0].shape[2]
    many = len(arrived)
    shards = tuple(k % (place.shape[0] - 1) for k in shards)
    items = [(g, s) for g in range(group) for s in range(many)]
    more = [] if start is None else [start]
    return pl.pallas_call(
        functools.partial(adjoint_kernel, first=first, items=items, shards=shards, fresh=start is None),
        out_shape=jax.ShapeDtypeStruct((group, u.shape[3] * u.shape[2], lines), F32),
        in_specs=[SMEM_SPEC, SMEM_SPEC, HBM_SPEC, HBM_SPEC] + [VMEM_SPEC] * (many + len(more)),
        out_specs=VMEM_SPEC,
        input_output_aliases={4 + many: 0} if more else {},
        scratch_shapes=buffers(len(items), rows, u),
        compiler_params=pltpu.CompilerParams(vmem_limit_bytes=VMEM),
        cost_estimate=cost(len(items), rows, u),
    )(place, ranks, u, v, *arrived, *more)


def ring_order(count):
    return [2 * k for k in range(count // 2)] + [2 * k + 1 for k in reversed(range(count // 2))]


class Rings:
    def __init__(self, col_count):
        order = ring_order(col_count)
        self.fore = [(order[k], order[(k + 1) % col_count]) for k in range(col_count)]
        self.back = [(b, a) for a, b in self.fore]
        ahead_of = [[order[(order.index(c) + k) % col_count] for k in range(col_count)] for c in range(col_count)]
        mine = lax.dynamic_slice(jnp.array(ahead_of, jnp.int32), (lax.axis_index("col"), 0), (1, col_count))
        self.table = jnp.concatenate([mine[0], lax.axis_index("row").astype(jnp.int32)[None]])

    def ahead(self, x):
        return lax.ppermute(x, "col", self.fore)

    def behind(self, x):
        return lax.ppermute(x, "col", self.back)


def swap_core(x):
    return lax.ppermute(x, "row", [(k, k ^ 1) for k in range(4)])


def swap_chip(x):
    return lax.ppermute(x, "row", [(k, k ^ 2) for k in range(4)])


def gather_model(half):
    across = swap_chip(half)
    beside = swap_core(half)
    corner = swap_core(across)
    return jnp.stack([half, beside, across, corner], 1)


def scatter_gradient(total):
    group, count, lines = total.shape
    row = lax.axis_index("row")
    core = row & 1
    chip = row >> 1
    shards = total.reshape(group, 2, 2, count // 4, lines)

    def pick(x, c):
        return lax.dynamic_slice(shards, (0, x, c, 0, 0), (group, 1, 1, count // 4, lines)).reshape(
            group, count // 4, lines
        )

    far = pick(1 - chip, core) + swap_core(pick(1 - chip, 1 - core).astype(BF16)).astype(F32)
    other = swap_chip(far.astype(BF16))
    near = pick(chip, core) + swap_core(pick(chip, 1 - core).astype(BF16)).astype(F32)
    return near, other


def local_ring(u, v, ranks, model_init, observed, step, *, col_count):
    frequencies, tile_rows, size, cols, width = u.shape
    rows = tile_rows // col_count
    rings = Rings(col_count)
    far = col_count // 2
    cut = rows * size // 2
    group = frequencies // GROUPS
    models, misfits = [], []
    for first in range(0, frequencies, group):
        some = slice(first, first + group)
        model = model_init[some]
        for sweep in range(ITERS):
            x = gather_model(model.astype(BF16))
            (part,) = forward(u, v, x, ranks, rings.table, (far,), first, rows, BF16)
            fore = rings.ahead(part[:, :cut])
            back = rings.behind(part[:, cut:])
            for k in range(far - 1, 0, -1):
                up, down = forward(u, v, x, ranks, rings.table, (k, -k), first, rows, F32)
                if k == far - 1:
                    up = jnp.concatenate([up[:, :cut] + fore.astype(F32), up[:, cut:]], 1)
                    down = jnp.concatenate([down[:, :cut], down[:, cut:] + back.astype(F32)], 1)
                else:
                    up = up + fore.astype(F32)
                    down = down + back.astype(F32)
                fore = rings.ahead(up.astype(BF16))
                back = rings.behind(down.astype(BF16))
            (own,) = forward(u, v, x, ranks, rings.table, (0,), first, rows, F32)
            misfit = own + fore.astype(F32) + back.astype(F32) - observed[some]
            half = misfit.astype(BF16)
            fore = rings.ahead(half)
            back = rings.behind(half)
            total = adjoint(u, v, [half], ranks, None, rings.table, (0,), first, rows)
            for k in range(1, far):
                arrived = [fore, back]
                if k < far - 1:
                    fore, back = rings.ahead(fore), rings.behind(back)
                else:
                    fore, back = rings.ahead(fore[:, :cut]), rings.behind(back[:, cut:])
                total = adjoint(u, v, arrived, ranks, total, rings.table, (-k, k), first, rows)
            last = jnp.concatenate([fore, back], 1)
            total = adjoint(u, v, [last], ranks, total, rings.table, (far,), first, rows)
            near, other = scatter_gradient(total)
            model = model - step[some, None, None] * (near + other.astype(F32))
        models.append(model)
        misfits.append(misfit)
    return (jnp.concatenate(models, 0), jnp.concatenate(misfits, 0))


def solution(mesh):
    col_count, row_count = mesh.shape["col"], mesh.shape["row"]

    def local(u, v, ranks, model_init, observed, step):
        if row_count == 4 and col_count % 2 == 0 and col_count >= 4 and u.shape[1] % col_count == 0:
            return local_ring(u, v, ranks, model_init, observed, step, col_count=col_count)
        return local_plain(u, v, ranks, model_init, observed, step)

    return jax.shard_map(
        local,
        mesh=mesh,
        in_specs=(
            P(None, "row", None, "col", None),
            P(None, "row", None, "col", None),
            P(None, "row", "col"),
            P(None, ("col", "row"), None),
            P(None, ("row", "col"), None),
            P(),
        ),
        out_specs=(P(None, ("col", "row"), None), P(None, ("row", "col"), None)),
        check_vma=False,
    )
```

time: 869 us -> 308 us (0.35)
  waiting for transfers between devices: 555 us -> 124 us
  matrix products: 116 us -> 0 us
  Pallas kernels: 0 us -> 116 us
  local copies, waits for them, and re-layouts: 92.9 us -> 3.92 us
  other arithmetic: 88.6 us -> 11.7 us
  starting transfers between devices: 0.73 us -> 44.6 us
  between operations: 14.3 us -> 1.48 us
    reduce_scatter x4 -> x0, waiting for transfers between devices: 387 us -> none  [the longest x2 301 us: local(): lax.psum_scatter(partial_value, 'col', scatter_dimension=1, tiled=True)]
    all_gather x4 -> x0, waiting for transfers between devices: 168 us -> none  [the longest x2 146 us: local(): lax.all_gather(misfit.astype(jnp.bfloat16), 'col', axis=1, tiled=True)]
    ppermute x0 -> x44, waiting for transfers between devices: none -> 124 us  [the longest x4 48.5 us: swap_chip(): return lax.ppermute(x, 'row', [(k, k ^ 2) for k in range(4)])]
    pallas_call x0 -> x20, Pallas kernels: none -> 116 us  [the longest x10 58.8 us: forward(): pl.pallas_call(functools.partial(forward_kernel, first=first, items=items...]
    unnamed x4 -> x0, matrix products: 69.6 us -> none
    dot_general x4 -> x0, matrix products: 46.4 us -> none  [the longest x2 24.4 us: local(): jnp.einsum('fiajk,fijkl->fial', u_factors, coefficient, preferred_element...]
    dot_general x2 -> x0, local copies, waits for them, and re-layouts: 45.8 us -> none  [local(): jnp.einsum('fiajk,fial->fijkl', u_factors, misfit_tiles, preferred_elemen...]
    ppermute x0 -> x44, starting transfers between devices: none -> 44.6 us  [the longest x16 26.7 us: ahead(): return lax.ppermute(x, 'col', self.fore)]
  transfers between devices with their start and end apart: 8 -> 44, of which waited for: 7 -> 21; matrix products, arithmetic and copies ran while one was open for 5% -> 2% of each run, Pallas kernels for 0% -> 33%
where the time goes in v1:
time: 308 us; the launch traced here: 302 us
  waiting for transfers between devices  124 us (40%)
  Pallas kernels  116 us (38%)
  starting transfers between devices  44.6 us (14%)
  other arithmetic  11.7 us (4%)
  local copies, waits for them, and re-layouts  3.92 us (1%)
    pallas_call x10, Pallas kernels, forward(): pl.pallas_call(functools.partial(forward_kernel, first=first, items=items...  58.8 us
    pallas_call x10, Pallas kernels, adjoint(): pl.pallas_call(functools.partial(adjoint_kernel, first=first, items=items...  57.7 us
    ppermute x4, waiting for transfers between devices, swap_chip(): return lax.ppermute(x, 'row', [(k, k ^ 2) for k in range(4)])  48.5 us
    ppermute x16, waiting for transfers between devices, ahead(): return lax.ppermute(x, 'col', self.fore)  36.2 us
    ppermute x16, waiting for transfers between devices, behind(): return lax.ppermute(x, 'col', self.back)  34.3 us
    ppermute x16, starting transfers between devices, ahead(): return lax.ppermute(x, 'col', self.fore)  26.7 us
    ppermute x16, starting transfers between devices, behind(): return lax.ppermute(x, 'col', self.back)  9 us
    ppermute x4, starting transfers between devices, swap_chip(): return lax.ppermute(x, 'row', [(k, k ^ 2) for k in range(4)])  7.72 us
  transfers between devices with their start and end apart: 44, of which 21 were waited for; matrix products, arithmetic and copies ran while one was open for 2% of the time, Pallas kernels for 33%

profile of v1, /device:TPU:0, one launch (start us, length us, event | category | flops | bytes accessed | tf_op | source)
XLA Modules:
  0.0 301.9 jit_solution(9670827144708536782)
XLA Ops:
  4.9 11.9 %collective-permute-done.1 = bf16[2,512,256]{2,1,0:T(8,128)(2,1)S(1)} collective-permute-done((bf16[2,512,256]{2,1,0:T(8,128)(2,1)S(1)}, bf16[2,512,256]{2,1,0:T(8,128)(2,1)S(1)}, u32[]{:S(2)}, u32[]{:S(2)}) %collective-permute-start.1) | collective-permute-done | bytes 524320 | tf_op jit(solution)/shard_map/ppermute | solution.py:247
  26.3 6.8 %shard_map.89 = (f32[2,512,256]{2,1,0:T(8,128)S(1)}, f32[2,512,256]{2,1,0:T(8,128)S(1)}) custom-call(s32[9]{0:T(128)S(1)} %pad_add_fusion.place, s32[2,16,8]{2,1,0:T(8,128)S(1)} %copy.57.ranks, bf16[2,4,512,256]{3,2,1,0:T(8,128)(2,1)S(1)} %pad_maximum_fusion.x_ref, bf16[2,16,256,8,128]{4,3,2,1,0:T(8,128)(2,1)} %u_hbm.39, bf16[2,16,256,8,128]{4,3,2,1,0:T(8,128)(2,1)} %v_hbm.39), custom_call_target="tpu_custom_call" | custom-call | flops 4294967296 | bytes 8388608 | tf_op jit(solution)/shard_map/pallas_call | solution.py:193
  35.5 6.2 %collective-permute-done.7 = bf16[2,256,256]{2,1,0:T(8,128)(2,1)S(1)} collective-permute-done((bf16[2,256,256]{2,1,0:T(8,128)(2,1)S(1)}, bf16[2,256,256]{2,1,0:T(8,128)(2,1)S(1)}, u32[]{:S(2)}, u32[]{:S(2)}) %collective-permute-start.7) | collective-permute-done | bytes 262176 | tf_op jit(solution)/shard_map/ppermute | solution.py:239
  42.6 6.8 %shard_map.88 = (f32[2,512,256]{2,1,0:T(8,128)S(1)}, f32[2,512,256]{2,1,0:T(8,128)S(1)}) custom-call(s32[9]{0:T(128)S(1)} %pad_add_fusion.place, s32[2,16,8]{2,1,0:T(8,128)S(1)} %copy.57.ranks, bf16[2,4,512,256]{3,2,1,0:T(8,128)(2,1)S(1)} %pad_maximum_fusion.x_ref, bf16[2,16,256,8,128]{4,3,2,1,0:T(8,128)(2,1)} %u_hbm.39, bf16[2,16,256,8,128]{4,3,2,1,0:T(8,128)(2,1)} %v_hbm.39), custom_call_target="tpu_custom_call" | custom-call | flops 4294967296 | bytes 8388608 | tf_op jit(solution)/shard_map/pallas_call | solution.py:193
  56.1 6.8 %shard_map.87 = (f32[2,512,256]{2,1,0:T(8,128)S(1)}, f32[2,512,256]{2,1,0:T(8,128)S(1)}) custom-call(s32[9]{0:T(128)S(1)} %pad_add_fusion.place, s32[2,16,8]{2,1,0:T(8,128)S(1)} %copy.57.ranks, bf16[2,4,512,256]{3,2,1,0:T(8,128)(2,1)S(1)} %pad_maximum_fusion.x_ref, bf16[2,16,256,8,128]{4,3,2,1,0:T(8,128)(2,1)} %u_hbm.39, bf16[2,16,256,8,128]{4,3,2,1,0:T(8,128)(2,1)} %v_hbm.39), custom_call_target="tpu_custom_call" | custom-call | flops 4294967296 | bytes 8388608 | tf_op jit(solution)/shard_map/pallas_call | solution.py:193
  82.1 10.1 %collective-permute-done.11.rest_0_ = bf16[2,512,256]{2,1,0:T(8,128)(2,1)S(1)} collective-permute-done((bf16[2,512,256]{2,1,0:T(8,128)(2,1)S(1)}, bf16[2,512,256]{2,1,0:T(8,128)(2,1)S(1)}, u32[]{:S(2)}, u32[]{:S(2)}) %collective-permute-start.11) | collective-permute-done | bytes 524320 | tf_op jit(solution)/shard_map/ppermute | solution.py:236
  98.5 5.8 %collective-permute-done.12.rest_0_ = bf16[2,512,256]{2,1,0:T(8,128)(2,1)S(1)} collective-permute-done((bf16[2,512,256]{2,1,0:T(8,128)(2,1)S(1)}, bf16[2,512,256]{2,1,0:T(8,128)(2,1)S(1)}, u32[]{:S(2)}, u32[]{:S(2)}) %collective-permute-start.12) | collective-permute-done | bytes 524320 | tf_op jit(solution)/shard_map/ppermute | solution.py:236
  106.3 6.6 %shard_map.92.rest_2_ = f32[2,2048,256]{2,1,0:T(8,128)S(1)} custom-call(s32[9]{0:T(128)S(1)} %pad_add_fusion.place, s32[2,16,8]{2,1,0:T(8,128)S(1)} %copy.57.ranks, bf16[2,16,256,8,128]{4,3,2,1,0:T(8,128)(2,1)} %u_hbm.39, bf16[2,16,256,8,128]{4,3,2,1,0:T(8,128)(2,1)} %v_hbm.39, ...), custom_call_target="tpu_custom_call", output_to_operand_aliasing={{}: (6, {})} | custom-call | flops 4294967296 | bytes 8388608 | tf_op jit(solution)/shard_map/pallas_call | solution.py:210
  112.9 6.6 %shard_map.93.rest_2_ = f32[2,2048,256]{2,1,0:T(8,128)S(1)} custom-call(s32[9]{0:T(128)S(1)} %pad_add_fusion.place, s32[2,16,8]{2,1,0:T(8,128)S(1)} %copy.57.ranks, bf16[2,16,256,8,128]{4,3,2,1,0:T(8,128)(2,1)} %u_hbm.39, bf16[2,16,256,8,128]{4,3,2,1,0:T(8,128)(2,1)} %v_hbm.39, ...), custom_call_target="tpu_custom_call", output_to_operand_aliasing={{}: (6, {})} | custom-call | flops 4294967296 | bytes 8388608 | tf_op jit(solution)/shard_map/pallas_call | solution.py:210
  122.0 6.7 %shard_map.94.rest_1_ = f32[2,2048,256]{2,1,0:T(8,128)S(1)} custom-call(s32[9]{0:T(128)S(1)} %pad_add_fusion.place, s32[2,16,8]{2,1,0:T(8,128)S(1)} %copy.57.ranks, bf16[2,16,256,8,128]{4,3,2,1,0:T(8,128)(2,1)} %u_hbm.39, bf16[2,16,256,8,128]{4,3,2,1,0:T(8,128)(2,1)} %v_hbm.39, ...), custom_call_target="tpu_custom_call", output_to_operand_aliasing={{}: (6, {})} | custom-call | flops 4294967296 | bytes 8388608 | tf_op jit(solution)/shard_map/pallas_call | solution.py:210
  128.7 4.6 %shard_map.95 = f32[2,2048,256]{2,1,0:T(8,128)S(1)} custom-call(s32[9]{0:T(128)S(1)} %pad_add_fusion.place, s32[2,16,8]{2,1,0:T(8,128)S(1)} %copy.57.ranks, bf16[2,16,256,8,128]{4,3,2,1,0:T(8,128)(2,1)} %u_hbm.39, bf16[2,16,256,8,128]{4,3,2,1,0:T(8,128)(2,1)} %v_hbm.39, ...), custom_call_target="tpu_custom_call", output_to_operand_aliasing={{}: (5, {})} | custom-call | flops 2147483648 | bytes 4194304 | tf_op jit(solution)/shard_map/pallas_call | solution.py:210
  140.3 12.5 %collective-permute-done.21 = bf16[2,512,256]{2,1,0:T(8,128)(2,1)S(1)} collective-permute-done((bf16[2,512,256]{2,1,0:T(8,128)(2,1)S(1)}, bf16[2,512,256]{2,1,0:T(8,128)(2,1)S(1)}, u32[]{:S(2)}, u32[]{:S(2)}) %collective-permute-start.21) | collective-permute-done | bytes 524320 | tf_op jit(solution)/shard_map/ppermute | solution.py:247
  155.9 11.6 %collective-permute-done.23 = bf16[2,512,256]{2,1,0:T(8,128)(2,1)S(1)} collective-permute-done((bf16[2,512,256]{2,1,0:T(8,128)(2,1)S(1)}, bf16[2,512,256]{2,1,0:T(8,128)(2,1)S(1)}, u32[]{:S(2)}, u32[]{:S(2)}) %collective-permute-start.23) | collective-permute-done | bytes 524320 | tf_op jit(solution)/shard_map/ppermute | solution.py:247
  176.2 6.8 %shard_map.99 = (f32[2,512,256]{2,1,0:T(8,128)S(1)}, f32[2,512,256]{2,1,0:T(8,128)S(1)}) custom-call(s32[9]{0:T(128)S(1)} %pad_add_fusion.place, s32[2,16,8]{2,1,0:T(8,128)S(1)} %copy.57.ranks, bf16[2,4,512,256]{3,2,1,0:T(8,128)(2,1)S(1)} %pad_maximum_fusion.1.x_ref, bf16[2,16,256,8,128]{4,3,2,1,0:T(8,128)(2,1)} %u_hbm.39, bf16[2,16,256,8,128]{4,3,2,1,0:T(8,128)(2,1)} %v_hbm.39), custom_call_target="tpu_custom_call" | custom-call | flops 4294967296 | bytes 8388608 | tf_op jit(solution)/shard_map/pallas_call | solution.py:193
  185.4 5.8 %collective-permute-done.29 = bf16[2,256,256]{2,1,0:T(8,128)(2,1)S(1)} collective-permute-done((bf16[2,256,256]{2,1,0:T(8,128)(2,1)S(1)}, bf16[2,256,256]{2,1,0:T(8,128)(2,1)S(1)}, u32[]{:S(2)}, u32[]{:S(2)}) %collective-permute-start.29) | collective-permute-done | bytes 262176 | tf_op jit(solution)/shard_map/ppermute | solution.py:239
  191.8 6.8 %shard_map.98 = (f32[2,512,256]{2,1,0:T(8,128)S(1)}, f32[2,512,256]{2,1,0:T(8,128)S(1)}) custom-call(s32[9]{0:T(128)S(1)} %pad_add_fusion.place, s32[2,16,8]{2,1,0:T(8,128)S(1)} %copy.57.ranks, bf16[2,4,512,256]{3,2,1,0:T(8,128)(2,1)S(1)} %pad_maximum_fusion.1.x_ref, bf16[2,16,256,8,128]{4,3,2,1,0:T(8,128)(2,1)} %u_hbm.39, bf16[2,16,256,8,128]{4,3,2,1,0:T(8,128)(2,1)} %v_hbm.39), custom_call_target="tpu_custom_call" | custom-call | flops 4294967296 | bytes 8388608 | tf_op jit(solution)/shard_map/pallas_call | solution.py:193
  205.0 6.8 %shard_map.97 = (f32[2,512,256]{2,1,0:T(8,128)S(1)}, f32[2,512,256]{2,1,0:T(8,128)S(1)}) custom-call(s32[9]{0:T(128)S(1)} %pad_add_fusion.place, s32[2,16,8]{2,1,0:T(8,128)S(1)} %copy.57.ranks, bf16[2,4,512,256]{3,2,1,0:T(8,128)(2,1)S(1)} %pad_maximum_fusion.1.x_ref, bf16[2,16,256,8,128]{4,3,2,1,0:T(8,128)(2,1)} %u_hbm.39, bf16[2,16,256,8,128]{4,3,2,1,0:T(8,128)(2,1)} %v_hbm.39), custom_call_target="tpu_custom_call" | custom-call | flops 4294967296 | bytes 8388608 | tf_op jit(solution)/shard_map/pallas_call | solution.py:193
  230.9 10.1 %collective-permute-done.33.rest_0_ = bf16[2,512,256]{2,1,0:T(8,128)(2,1)S(1)} collective-permute-done((bf16[2,512,256]{2,1,0:T(8,128)(2,1)S(1)}, bf16[2,512,256]{2,1,0:T(8,128)(2,1)S(1)}, u32[]{:S(2)}, u32[]{:S(2)}) %collective-permute-start.33) | collective-permute-done | bytes 524320 | tf_op jit(solution)/shard_map/ppermute | solution.py:236
  247.3 6.0 %collective-permute-done.34.rest_0_ = bf16[2,512,256]{2,1,0:T(8,128)(2,1)S(1)} collective-permute-done((bf16[2,512,256]{2,1,0:T(8,128)(2,1)S(1)}, bf16[2,512,256]{2,1,0:T(8,128)(2,1)S(1)}, u32[]{:S(2)}, u32[]{:S(2)}) %collective-permute-start.34) | collective-permute-done | bytes 524320 | tf_op jit(solution)/shard_map/ppermute | solution.py:236
  255.6 6.7 %shard_map.102.rest_2_ = f32[2,2048,256]{2,1,0:T(8,128)S(1)} custom-call(s32[9]{0:T(128)S(1)} %pad_add_fusion.place, s32[2,16,8]{2,1,0:T(8,128)S(1)} %copy.57.ranks, bf16[2,16,256,8,128]{4,3,2,1,0:T(8,128)(2,1)} %u_hbm.39, bf16[2,16,256,8,128]{4,3,2,1,0:T(8,128)(2,1)} %v_hbm.39, ...), custom_call_target="tpu_custom_call", output_to_operand_aliasing={{}: (6, {})} | custom-call | flops 4294967296 | bytes 8388608 | tf_op jit(solution)/shard_map/pallas_call | solution.py:210
  262.2 6.7 %shard_map.103.rest_2_ = f32[2,2048,256]{2,1,0:T(8,128)S(1)} custom-call(s32[9]{0:T(128)S(1)} %pad_add_fusion.place, s32[2,16,8]{2,1,0:T(8,128)S(1)} %copy.57.ranks, bf16[2,16,256,8,128]{4,3,2,1,0:T(8,128)(2,1)} %u_hbm.39, bf16[2,16,256,8,128]{4,3,2,1,0:T(8,128)(2,1)} %v_hbm.39, ...), custom_call_target="tpu_custom_call", output_to_operand_aliasing={{}: (6, {})} | custom-call | flops 4294967296 | bytes 8388608 | tf_op jit(solution)/shard_map/pallas_call | solution.py:210
  271.4 6.7 %shard_map.104.rest_1_ = f32[2,2048,256]{2,1,0:T(8,128)S(1)} custom-call(s32[9]{0:T(128)S(1)} %pad_add_fusion.place, s32[2,16,8]{2,1,0:T(8,128)S(1)} %copy.57.ranks, bf16[2,16,256,8,128]{4,3,2,1,0:T(8,128)(2,1)} %u_hbm.39, bf16[2,16,256,8,128]{4,3,2,1,0:T(8,128)(2,1)} %v_hbm.39, ...), custom_call_target="tpu_custom_call", output_to_operand_aliasing={{}: (6, {})} | custom-call | flops 4294967296 | bytes 8388608 | tf_op jit(solution)/shard_map/pallas_call | solution.py:210
  278.1 4.6 %shard_map.105 = f32[2,2048,256]{2,1,0:T(8,128)S(1)} custom-call(s32[9]{0:T(128)S(1)} %pad_add_fusion.place, s32[2,16,8]{2,1,0:T(8,128)S(1)} %copy.57.ranks, bf16[2,16,256,8,128]{4,3,2,1,0:T(8,128)(2,1)} %u_hbm.39, bf16[2,16,256,8,128]{4,3,2,1,0:T(8,128)(2,1)} %v_hbm.39, ...), custom_call_target="tpu_custom_call", output_to_operand_aliasing={{}: (5, {})} | custom-call | flops 2147483648 | bytes 4194304 | tf_op jit(solution)/shard_map/pallas_call | solution.py:210
  286.5 12.5 %collective-permute-done.43 = bf16[2,512,256]{2,1,0:T(8,128)(2,1)S(1)} collective-permute-done((bf16[2,512,256]{2,1,0:T(8,128)(2,1)S(1)}, bf16[2,512,256]{2,1,0:T(8,128)(2,1)S(1)}, u32[]{:S(2)}, u32[]{:S(2)}) %collective-permute-start.43) | collective-permute-done | bytes 524320 | tf_op jit(solution)/shard_map/ppermute | solution.py:247
  (137 shorter events, 117.9 us)
Async XLA Ops:
  1.9 14.9 %collective-permute-start.1 = (bf16[2,512,256]{2,1,0:T(8,128)(2,1)S(1)}, bf16[2,512,256]{2,1,0:T(8,128)(2,1)S(1)}, u32[]{:S(2)}, u32[]{:S(2)}) collective-permute-start(bf16[2,512,256]{2,1,0:T(8,128)(2,1)S(1)} %convert_element_type.136), channel_id=1, source_target_pairs={{0,2},{1,3},{2,0},{3,1},{4,6},{5,7},{6,4},{7,5},{8,10},{9,11},{10,... | collective-permute-start | bytes 1572872 | tf_op jit(solution)/shard_map/ppermute | solution.py:247
  4.9 14.8 %collective-permute-start = (bf16[2,512,256]{2,1,0:T(8,128)(2,1)S(1)}, bf16[2,512,256]{2,1,0:T(8,128)(2,1)S(1)}, u32[]{:S(2)}, u32[]{:S(2)}) collective-permute-start(bf16[2,512,256]{2,1,0:T(8,128)(2,1)S(1)} %convert_element_type.136), channel_id=1, source_target_pairs={{0,1},{1,0},{2,3},{3,2},{4,5},{5,4},{6,7},{7,6},{8,9},{9,8},{10,11... | collective-permute-start | bytes 1572872 | tf_op jit(solution)/shard_map/ppermute | solution.py:243
  33.6 15.8 %collective-permute-start.4 = (bf16[2,512,256]{2,1,0:T(8,128)(2,1)S(1)}, bf16[2,512,256]{2,1,0:T(8,128)(2,1)S(1)}, u32[]{:S(2)}, u32[]{:S(2)}) collective-permute-start(bf16[2,512,256]{2,1,0:T(8,128)(2,1)S(1)} %pad_maximum_fusion.2), channel_id=1, source_target_pairs={{0,8},{8,16},{16,24},{24,28},{28,20},{20,12},{12,4},{4,0},{1,9},{9... | collective-permute-start | bytes 1572872 | tf_op jit(solution)/shard_map/ppermute | solution.py:236
  41.8 13.7 %collective-permute-start.8 = (bf16[2,512,256]{2,1,0:T(8,128)(2,1)S(1)}, bf16[2,512,256]{2,1,0:T(8,128)(2,1)S(1)}, u32[]{:S(2)}, u32[]{:S(2)}) collective-permute-start(bf16[2,512,256]{2,1,0:T(8,128)(2,1)S(1)} %pad_maximum_fusion.3), channel_id=1, source_target_pairs={{8,0},{16,8},{24,16},{28,24},{20,28},{12,20},{4,12},{0,4},{9,1},{1... | collective-permute-start | bytes 1572872 | tf_op jit(solution)/shard_map/ppermute | solution.py:239
  49.6 13.4 %collective-permute-start.5 = (bf16[2,512,256]{2,1,0:T(8,128)(2,1)S(1)}, bf16[2,512,256]{2,1,0:T(8,128)(2,1)S(1)}, u32[]{:S(2)}, u32[]{:S(2)}) collective-permute-start(bf16[2,512,256]{2,1,0:T(8,128)(2,1)S(1)} %add_convert_fusion.7), channel_id=1, source_target_pairs={{0,8},{8,16},{16,24},{24,28},{28,20},{20,12},{12,4},{4,0},{1,9},{9... | collective-permute-start | bytes 1572872 | tf_op jit(solution)/shard_map/ppermute | solution.py:236
  55.7 12.4 %collective-permute-start.9 = (bf16[2,512,256]{2,1,0:T(8,128)(2,1)S(1)}, bf16[2,512,256]{2,1,0:T(8,128)(2,1)S(1)}, u32[]{:S(2)}, u32[]{:S(2)}) collective-permute-start(bf16[2,512,256]{2,1,0:T(8,128)(2,1)S(1)} %add_convert_fusion.5), channel_id=1, source_target_pairs={{8,0},{16,8},{24,16},{28,24},{20,28},{12,20},{4,12},{0,4},{9,1},{1... | collective-permute-start | bytes 1572872 | tf_op jit(solution)/shard_map/ppermute | solution.py:239
  63.1 12.2 %collective-permute-start.6 = (bf16[2,512,256]{2,1,0:T(8,128)(2,1)S(1)}, bf16[2,512,256]{2,1,0:T(8,128)(2,1)S(1)}, u32[]{:S(2)}, u32[]{:S(2)}) collective-permute-start(bf16[2,512,256]{2,1,0:T(8,128)(2,1)S(1)} %add_convert_fusion.6), channel_id=1, source_target_pairs={{0,8},{8,16},{16,24},{24,28},{28,20},{20,12},{12,4},{4,0},{1,9},{9... | collective-permute-start | bytes 1572872 | tf_op jit(solution)/shard_map/ppermute | solution.py:236
  79.9 12.3 %collective-permute-start.11 = (bf16[2,512,256]{2,1,0:T(8,128)(2,1)S(1)}, bf16[2,512,256]{2,1,0:T(8,128)(2,1)S(1)}, u32[]{:S(2)}, u32[]{:S(2)}) collective-permute-start(bf16[2,512,256]{2,1,0:T(8,128)(2,1)S(1)} %subtract_convert_fusion.rest_0_), channel_id=1, source_target_pairs={{0,8},{8,16},{16,24},{24,28},{28,20},{20,12},{12,4},{4,0},{1,9},{9... | collective-permute-start | bytes 1572872 | tf_op jit(solution)/shard_map/ppermute | solution.py:236
  81.7 12.1 %collective-permute-start.15 = (bf16[2,512,256]{2,1,0:T(8,128)(2,1)S(1)}, bf16[2,512,256]{2,1,0:T(8,128)(2,1)S(1)}, u32[]{:S(2)}, u32[]{:S(2)}) collective-permute-start(bf16[2,512,256]{2,1,0:T(8,128)(2,1)S(1)} %subtract_convert_fusion.rest_0_), channel_id=1, source_target_pairs={{8,0},{16,8},{24,16},{28,24},{20,28},{12,20},{4,12},{0,4},{9,1},{1... | collective-permute-start | bytes 1572872 | tf_op jit(solution)/shard_map/ppermute | solution.py:239
  92.2 12.1 %collective-permute-start.12 = (bf16[2,512,256]{2,1,0:T(8,128)(2,1)S(1)}, bf16[2,512,256]{2,1,0:T(8,128)(2,1)S(1)}, u32[]{:S(2)}, u32[]{:S(2)}) collective-permute-start(bf16[2,512,256]{2,1,0:T(8,128)(2,1)S(1)} %collective-permute-done.11.rest_0_), channel_id=1, source_target_pairs={{0,8},{8,16},{16,24},{24,28},{28,20},{20,12},{12,4},{4,0},{1,9},{9... | collective-permute-start | bytes 1572872 | tf_op jit(solution)/shard_map/ppermute | solution.py:236
  93.8 12.1 %collective-permute-start.16 = (bf16[2,512,256]{2,1,0:T(8,128)(2,1)S(1)}, bf16[2,512,256]{2,1,0:T(8,128)(2,1)S(1)}, u32[]{:S(2)}, u32[]{:S(2)}) collective-permute-start(bf16[2,512,256]{2,1,0:T(8,128)(2,1)S(1)} %collective-permute-done.15.rest_1_), channel_id=1, source_target_pairs={{8,0},{16,8},{24,16},{28,24},{20,28},{12,20},{4,12},{0,4},{9,1},{1... | collective-permute-start | bytes 1572872 | tf_op jit(solution)/shard_map/ppermute | solution.py:239
  104.3 15.3 %collective-permute-start.13 = (bf16[2,512,256]{2,1,0:T(8,128)(2,1)S(1)}, bf16[2,512,256]{2,1,0:T(8,128)(2,1)S(1)}, u32[]{:S(2)}, u32[]{:S(2)}) collective-permute-start(bf16[2,512,256]{2,1,0:T(8,128)(2,1)S(1)} %collective-permute-done.12.rest_0_), channel_id=1, source_target_pairs={{0,8},{8,16},{16,24},{24,28},{28,20},{20,12},{12,4},{4,0},{1,9},{9... | collective-permute-start | bytes 1572872 | tf_op jit(solution)/shard_map/ppermute | solution.py:236
  105.9 15.4 %collective-permute-start.17 = (bf16[2,512,256]{2,1,0:T(8,128)(2,1)S(1)}, bf16[2,512,256]{2,1,0:T(8,128)(2,1)S(1)}, u32[]{:S(2)}, u32[]{:S(2)}) collective-permute-start(bf16[2,512,256]{2,1,0:T(8,128)(2,1)S(1)} %collective-permute-done.16.rest_1_), channel_id=1, source_target_pairs={{8,0},{16,8},{24,16},{28,24},{20,28},{12,20},{4,12},{0,4},{9,1},{1... | collective-permute-start | bytes 1572872 | tf_op jit(solution)/shard_map/ppermute | solution.py:239
  138.8 14.0 %collective-permute-start.21 = (bf16[2,512,256]{2,1,0:T(8,128)(2,1)S(1)}, bf16[2,512,256]{2,1,0:T(8,128)(2,1)S(1)}, u32[]{:S(2)}, u32[]{:S(2)}) collective-permute-start(bf16[2,512,256]{2,1,0:T(8,128)(2,1)S(1)} %fusion.4), channel_id=1, source_target_pairs={{0,2},{1,3},{2,0},{3,1},{4,6},{5,7},{6,4},{7,5},{8,10},{9,11},{10,... | collective-permute-start | bytes 1572872 | tf_op jit(solution)/shard_map/ppermute | solution.py:247
  154.3 13.2 %collective-permute-start.23 = (bf16[2,512,256]{2,1,0:T(8,128)(2,1)S(1)}, bf16[2,512,256]{2,1,0:T(8,128)(2,1)S(1)}, u32[]{:S(2)}, u32[]{:S(2)}) collective-permute-start(bf16[2,512,256]{2,1,0:T(8,128)(2,1)S(1)} %fusion.13), channel_id=1, source_target_pairs={{0,2},{1,3},{2,0},{3,1},{4,6},{5,7},{6,4},{7,5},{8,10},{9,11},{10,... | collective-permute-start | bytes 1572872 | tf_op jit(solution)/shard_map/ppermute | solution.py:247
  183.8 14.9 %collective-permute-start.26 = (bf16[2,512,256]{2,1,0:T(8,128)(2,1)S(1)}, bf16[2,512,256]{2,1,0:T(8,128)(2,1)S(1)}, u32[]{:S(2)}, u32[]{:S(2)}) collective-permute-start(bf16[2,512,256]{2,1,0:T(8,128)(2,1)S(1)} %pad_maximum_fusion.5), channel_id=1, source_target_pairs={{0,8},{8,16},{16,24},{24,28},{28,20},{20,12},{12,4},{4,0},{1,9},{9... | collective-permute-start | bytes 1572872 | tf_op jit(solution)/shard_map/ppermute | solution.py:236
  191.3 12.9 %collective-permute-start.30 = (bf16[2,512,256]{2,1,0:T(8,128)(2,1)S(1)}, bf16[2,512,256]{2,1,0:T(8,128)(2,1)S(1)}, u32[]{:S(2)}, u32[]{:S(2)}) collective-permute-start(bf16[2,512,256]{2,1,0:T(8,128)(2,1)S(1)} %pad_maximum_fusion.6), channel_id=1, source_target_pairs={{8,0},{16,8},{24,16},{28,24},{20,28},{12,20},{4,12},{0,4},{9,1},{1... | collective-permute-start | bytes 1572872 | tf_op jit(solution)/shard_map/ppermute | solution.py:239
  198.8 13.0 %collective-permute-start.27 = (bf16[2,512,256]{2,1,0:T(8,128)(2,1)S(1)}, bf16[2,512,256]{2,1,0:T(8,128)(2,1)S(1)}, u32[]{:S(2)}, u32[]{:S(2)}) collective-permute-start(bf16[2,512,256]{2,1,0:T(8,128)(2,1)S(1)} %add_convert_fusion.3), channel_id=1, source_target_pairs={{0,8},{8,16},{16,24},{24,28},{28,20},{20,12},{12,4},{4,0},{1,9},{9... | collective-permute-start | bytes 1572872 | tf_op jit(solution)/shard_map/ppermute | solution.py:236
  204.3 12.1 %collective-permute-start.31 = (bf16[2,512,256]{2,1,0:T(8,128)(2,1)S(1)}, bf16[2,512,256]{2,1,0:T(8,128)(2,1)S(1)}, u32[]{:S(2)}, u32[]{:S(2)}) collective-permute-start(bf16[2,512,256]{2,1,0:T(8,128)(2,1)S(1)} %add_convert_fusion.1), channel_id=1, source_target_pairs={{8,0},{16,8},{24,16},{28,24},{20,28},{12,20},{4,12},{0,4},{9,1},{1... | collective-permute-start | bytes 1572872 | tf_op jit(solution)/shard_map/ppermute | solution.py:239
  230.5 12.1 %collective-permute-start.37 = (bf16[2,512,256]{2,1,0:T(8,128)(2,1)S(1)}, bf16[2,512,256]{2,1,0:T(8,128)(2,1)S(1)}, u32[]{:S(2)}, u32[]{:S(2)}) collective-permute-start(bf16[2,512,256]{2,1,0:T(8,128)(2,1)S(1)} %get-tuple-element.26.rest_0_), channel_id=1, source_target_pairs={{8,0},{16,8},{24,16},{28,24},{20,28},{12,20},{4,12},{0,4},{9,1},{1... | collective-permute-start | bytes 1572872 | tf_op jit(solution)/shard_map/ppermute | solution.py:239
  241.0 12.4 %collective-permute-start.34 = (bf16[2,512,256]{2,1,0:T(8,128)(2,1)S(1)}, bf16[2,512,256]{2,1,0:T(8,128)(2,1)S(1)}, u32[]{:S(2)}, u32[]{:S(2)}) collective-permute-start(bf16[2,512,256]{2,1,0:T(8,128)(2,1)S(1)} %collective-permute-done.33.rest_0_), channel_id=1, source_target_pairs={{0,8},{8,16},{16,24},{24,28},{28,20},{20,12},{12,4},{4,0},{1,9},{9... | collective-permute-start | bytes 1572872 | tf_op jit(solution)/shard_map/ppermute | solution.py:236
  253.3 15.6 %collective-permute-start.35 = (bf16[2,512,256]{2,1,0:T(8,128)(2,1)S(1)}, bf16[2,512,256]{2,1,0:T(8,128)(2,1)S(1)}, u32[]{:S(2)}, u32[]{:S(2)}) collective-permute-start(bf16[2,512,256]{2,1,0:T(8,128)(2,1)S(1)} %collective-permute-done.34.rest_0_), channel_id=1, source_target_pairs={{0,8},{8,16},{16,24},{24,28},{28,20},{20,12},{12,4},{4,0},{1,9},{9... | collective-permute-start | bytes 1572872 | tf_op jit(solution)/shard_map/ppermute | solution.py:236
  254.7 15.7 %collective-permute-start.39 = (bf16[2,512,256]{2,1,0:T(8,128)(2,1)S(1)}, bf16[2,512,256]{2,1,0:T(8,128)(2,1)S(1)}, u32[]{:S(2)}, u32[]{:S(2)}) collective-permute-start(bf16[2,512,256]{2,1,0:T(8,128)(2,1)S(1)} %collective-permute-done.38.rest_1_), channel_id=1, source_target_pairs={{8,0},{16,8},{24,16},{28,24},{20,28},{12,20},{4,12},{0,4},{9,1},{1... | collective-permute-start | bytes 1572872 | tf_op jit(solution)/shard_map/ppermute | solution.py:239
  285.0 14.0 %collective-permute-start.43 = (bf16[2,512,256]{2,1,0:T(8,128)(2,1)S(1)}, bf16[2,512,256]{2,1,0:T(8,128)(2,1)S(1)}, u32[]{:S(2)}, u32[]{:S(2)}) collective-permute-start(bf16[2,512,256]{2,1,0:T(8,128)(2,1)S(1)} %fusion), channel_id=1, source_target_pairs={{0,2},{1,3},{2,0},{3,1},{4,6},{5,7},{6,4},{7,5},{8,10},{9,11},{10,... | collective-permute-start | bytes 1572872 | tf_op jit(solution)/shard_map/ppermute | solution.py:247
  (25 other events, 219.0 us)
